TPU v7x, 32 devices: a whole 2x2x4 slice. The times are simulated.
32 devices in a mesh: grp: 4 (over x, core), dev: 8 (over z, y).
Axes of the slice: x: 2, y: 2, z: 4, core: 2. Of those that a mesh axis runs over, the one named last changes fastest.
Arguments:
- amplitudes: bfloat16 [32, 128, 128], P(('grp', 'dev')), may hold values from -2 to 2
- bases: bfloat16 [32, 256, 128], P(('grp', 'dev')), may hold values from -0.375 to 0.375
- factors: bfloat16 [32, 32, 256, 256], P(('grp', 'dev')), may hold values from -0.1875 to 0.1875
- intersections: bfloat16 [32, 4, 128, 128], P(('grp', 'dev')), may hold values from -0.25 to 0.25
- pair_integrals: float32 [32, 128, 128], P(('grp', 'dev')), may hold values from -6 to 6
- pno_energies: float32 [32, 128], P(('grp', 'dev')), may hold values from 0.3 to 3
- pair_shift: float32 [32], P(('grp', 'dev')), may hold values from 0.5 to 4
- pair_atoms: int32 [32, 2], P('grp'), may hold values from 0 to 7, all different within a row; in each aligned block of 8 rows (0 to 7, 8 to 15, ...) at most 3 rows name the same one
- pair_next: int32 [32, 4], P(('grp', 'dev')), may hold values from 0 to 15, as said below
Outputs:
- new_amplitudes: float32 [32, 128, 128], P(('grp', 'dev'))
Inputs may be any that keep to these rules, and one draw needn't show every extreme that they name: `pair_atoms`: each pair lists 2 different atoms of its own group. Within a group no atom is listed by more than 3 pairs, and some atom is listed by exactly 3 pairs of its group. `pair_next`: each pair lists 4 different pairs other than itself; a number below 8 is a pair of its own group, a number m from 8 on is pair m - 8 of the next group. Pairs of the last group list only pairs of their own group.
All inputs are finite; a program needn't handle non-finite values.
Results may differ from a plain program's by a relative error of at most 0.008.
Values may be sent and summed in bfloat16 or wider, within the bound.
No kernel may reach another device: no remote copies, remote signals or barrier semaphores. Data moves between devices by JAX's collectives and lax.ppermute only.
A program may use at most 128 MiB of HBM per device.

v0:
```python
import jax
import jax.numpy as jnp
from jax import lax
from jax.sharding import PartitionSpec as P

CAP = 3
ITERS = 2


def from_behind(value, axis, steps):
    count = lax.axis_size(axis)
    first, last = (max(0, -steps), min(count, count - steps))
    return lax.ppermute(value, axis, [(source, source + steps) for source in range(first, last)])


def expand(pair_bases, pair_amps):
    halfway = jnp.einsum(
        "nai,nij->naj", pair_bases, pair_amps, preferred_element_type=jnp.float32
    ).astype(jnp.bfloat16)
    return jnp.einsum(
        "naj,nbj->nab", halfway, pair_bases, preferred_element_type=jnp.float32
    ).astype(jnp.bfloat16)


def sandwich(factor_block, expanded):
    aux_count = factor_block.shape[0]
    pao_width = factor_block.shape[1]
    flat_factor = factor_block.reshape(aux_count * pao_width, pao_width)
    squeezed = jnp.dot(flat_factor, expanded, preferred_element_type=jnp.float32).astype(
        jnp.bfloat16
    )
    squeezed = squeezed.reshape(aux_count, pao_width, pao_width)
    return jnp.einsum("kad,kbd->ab", squeezed, factor_block, preferred_element_type=jnp.float32)


def select_rows(selector, stacked):
    flat_rows = stacked.reshape(stacked.shape[0], -1)
    picked = jnp.dot(selector, flat_rows, preferred_element_type=jnp.float32).astype(jnp.bfloat16)
    return picked.reshape((selector.shape[0],) + stacked.shape[1:])


def spread_terms(selector, terms):
    return jnp.dot(
        selector.T, terms, precision=lax.Precision.HIGHEST, preferred_element_type=jnp.float32
    )


def on_device(
    amplitudes,
    bases,
    factors,
    intersections,
    pair_integrals,
    pno_energies,
    pair_shift,
    pair_atoms,
    pair_next,
):
    local_atom = lax.axis_index("dev")
    group_size = lax.axis_size("dev")
    npno = amplitudes.shape[1]
    listed = jnp.sum((pair_atoms == local_atom).astype(jnp.int32), axis=1)
    earlier = jnp.cumsum(listed) - listed
    slot_ids = lax.iota(jnp.int32, CAP)
    selector = ((listed[None, :] == 1) & (earlier[None, :] == slot_ids[:, None])).astype(
        jnp.float32
    )
    selector_narrow = selector.astype(jnp.bfloat16)
    factor_block = factors[0]
    denominator = pno_energies[0][:, None] + pno_energies[0][None, :] + pair_shift[0]
    positions = lax.iota(jnp.int32, 2 * group_size)
    picker = (pair_next[0][:, None] == positions[None, :]).astype(jnp.bfloat16)
    pair_intersections = intersections[0]
    group_base = lax.all_gather(bases, "dev", axis=0, tiled=True)
    slot_bases = select_rows(selector_narrow, group_base)
    slot_wide = slot_bases.astype(jnp.float32)
    current = amplitudes
    update = None
    for iteration in range(ITERS):
        group_amps = lax.all_gather(current, "dev", axis=0, tiled=True)
        slot_amps = select_rows(selector_narrow, group_amps)
        ladder_slots = lax.map(
            lambda expanded: sandwich(factor_block, expanded), expand(slot_bases, slot_amps)
        )
        left_side = jnp.einsum(
            "nai,nab->nib", slot_wide, ladder_slots, precision=lax.Precision.HIGHEST
        )
        projected = jnp.einsum(
            "nib,nbj->nij", left_side, slot_wide, precision=lax.Precision.HIGHEST
        )
        terms = projected.reshape(CAP, npno * npno)
        arrived = lax.all_to_all(
            spread_terms(selector, terms), "dev", split_axis=0, concat_axis=0, tiled=True
        )
        summed = jnp.sum(arrived, axis=0).reshape(npno, npno)
        next_amps = from_behind(group_amps, "grp", -1)
        candidates = jnp.concatenate([group_amps, next_amps], axis=0)
        neighbours = select_rows(picker, candidates)
        mixed = jnp.einsum(
            "nij,njk->nik", pair_intersections, neighbours, preferred_element_type=jnp.float32
        ).astype(jnp.bfloat16)
        coupling = jnp.einsum(
            "nik,nlk->il", mixed, pair_intersections, preferred_element_type=jnp.float32
        )
        update = -(pair_integrals[0] + summed + coupling) / denominator
        if iteration + 1 < ITERS:
            current = update.astype(jnp.bfloat16)[None]
    return update[None]


def solution(mesh):
    return jax.shard_map(
        on_device,
        mesh=mesh,
        in_specs=(
            P(("grp", "dev"), None, None),
            P(("grp", "dev"), None, None),
            P(("grp", "dev"), None, None, None),
            P(("grp", "dev"), None, None, None),
            P(("grp", "dev"), None, None),
            P(("grp", "dev"), None),
            P(("grp", "dev")),
            P("grp", None),
            P(("grp", "dev"), None),
        ),
        out_specs=P(("grp", "dev"), None, None),
        check_vma=False,
    )
```

profile of v0, /device:TPU:0, one launch (start us, length us, event | category | flops | bytes accessed | tf_op | source)
XLA Modules:
  0.0 330.4 jit_solution(12958987099648264930)
XLA Ops:
  0.0 32.9 %all_gather.10 = bf16[8,128,128]{2,1,0:T(8,128)(2,1)S(1)} all-gather(bf16[1,128,128]{2,1,0:T(8,128)(2,1)} %param.13), channel_id=1, replica_groups=mesh['grp'=4,'dev'=8] {'dev'}, dimensions={0}, use_global_device_ids=true | all-gather | bytes 294912 | tf_op jit(solution)/shard_map/all_gather | solution.py:80
  33.8 31.4 %all_gather.9 = bf16[8,256,128]{2,1,0:T(8,128)(2,1)S(1)} all-gather(bf16[1,256,128]{2,1,0:T(8,128)(2,1)} %param.14), channel_id=1, replica_groups=mesh['grp'=4,'dev'=8] {'dev'}, dimensions={0}, use_global_device_ids=true | all-gather | bytes 589824 | tf_op jit(solution)/shard_map/all_gather | solution.py:74
  66.3 97.5 %while.20 = (s32[]{:T(128)}, f32[3,256,256]{2,1,0:T(8,128)S(1)}, bf16[3,256,256]{2,1,0:T(8,128)(2,1)S(1)}, bf16[1,32,256,256]{3,2,1,0:T(8,128)(2,1)}, bf16[32,256,256]{2,1,0:T(8,128)(2,1)}, /*index=5*/s32[]{:T(128)}) while((s32[]{:T(128)}, f32[3,256,256]{2,1,0:T(8,128)S(1)}, bf16[3,256,256]{2,1,0:T(8,128)(2,1)S(1)}, ...), condition=%wide.region_3.4_spmd, body=%wide.region_2.3_spmd.sunk | while | flops 2149580800 | bytes 42336340 | solution.py:82
  66.3 5.5 %fusion.112 = bf16[8192,256]{0,1:T(8,128)(2,1)} fusion(bf16[8192,256]{1,0:T(8,128)(2,1)} %bitcast.219, bf16[3,256,256]{2,1,0:T(8,128)(2,1)S(1)} %get-tuple-element.157, s32[]{:T(128)S(6)} %copy.123), kind=kOutput, calls=%fused_computation.1.clone.1 | convolution fusion | flops 1075838976 | bytes 8519684 | tf_op jit(solution)/shard_map/while/body/eval_jaxpr/dot_general | solution.py:29
  71.8 6.4 %copy.113 = bf16[8192,256]{1,0:T(8,128)(2,1)} copy(bf16[8192,256]{0,1:T(8,128)(2,1)} %fusion.112) | data formatting | bytes 8388608 | tf_op jit(solution)/shard_map/while/body/eval_jaxpr/reshape | solution.py:32
  78.2 7.9 %copy.114 = bf16[32,256,256]{1,0,2:T(8,128)(2,1)} copy(bf16[32,256,256]{2,1,0:T(8,128)(2,1)} %bitcast.224) | data formatting | bytes 8388608 | tf_op jit(solution)/shard_map/while/body/eval_jaxpr/reshape | solution.py:32
  86.1 7.9 %copy.115 = bf16[32,256,256]{1,0,2:T(8,128)(2,1)} copy(bf16[32,256,256]{2,1,0:T(8,128)(2,1)} %get-tuple-element.159) | data formatting | bytes 8388608 | tf_op jit(solution)/shard_map
  98.8 5.5 %fusion.112 = bf16[8192,256]{0,1:T(8,128)(2,1)} fusion(bf16[8192,256]{1,0:T(8,128)(2,1)} %bitcast.219, bf16[3,256,256]{2,1,0:T(8,128)(2,1)S(1)} %get-tuple-element.157, s32[]{:T(128)S(6)} %copy.123), kind=kOutput, calls=%fused_computation.1.clone.1 | convolution fusion | flops 1075838976 | bytes 8519684 | tf_op jit(solution)/shard_map/while/body/eval_jaxpr/dot_general | solution.py:29
  104.3 6.4 %copy.113 = bf16[8192,256]{1,0:T(8,128)(2,1)} copy(bf16[8192,256]{0,1:T(8,128)(2,1)} %fusion.112) | data formatting | bytes 8388608 | tf_op jit(solution)/shard_map/while/body/eval_jaxpr/reshape | solution.py:32
  110.7 7.9 %copy.114 = bf16[32,256,256]{1,0,2:T(8,128)(2,1)} copy(bf16[32,256,256]{2,1,0:T(8,128)(2,1)} %bitcast.224) | data formatting | bytes 8388608 | tf_op jit(solution)/shard_map/while/body/eval_jaxpr/reshape | solution.py:32
  118.6 7.9 %copy.115 = bf16[32,256,256]{1,0,2:T(8,128)(2,1)} copy(bf16[32,256,256]{2,1,0:T(8,128)(2,1)} %get-tuple-element.159) | data formatting | bytes 8388608 | tf_op jit(solution)/shard_map
  131.3 5.5 %fusion.112 = bf16[8192,256]{0,1:T(8,128)(2,1)} fusion(bf16[8192,256]{1,0:T(8,128)(2,1)} %bitcast.219, bf16[3,256,256]{2,1,0:T(8,128)(2,1)S(1)} %get-tuple-element.157, s32[]{:T(128)S(6)} %copy.123), kind=kOutput, calls=%fused_computation.1.clone.1 | convolution fusion | flops 1075838976 | bytes 8519684 | tf_op jit(solution)/shard_map/while/body/eval_jaxpr/dot_general | solution.py:29
  136.8 6.4 %copy.113 = bf16[8192,256]{1,0:T(8,128)(2,1)} copy(bf16[8192,256]{0,1:T(8,128)(2,1)} %fusion.112) | data formatting | bytes 8388608 | tf_op jit(solution)/shard_map/while/body/eval_jaxpr/reshape | solution.py:32
  143.2 7.9 %copy.114 = bf16[32,256,256]{1,0,2:T(8,128)(2,1)} copy(bf16[32,256,256]{2,1,0:T(8,128)(2,1)} %bitcast.224) | data formatting | bytes 8388608 | tf_op jit(solution)/shard_map/while/body/eval_jaxpr/reshape | solution.py:32
  151.1 7.9 %copy.115 = bf16[32,256,256]{1,0,2:T(8,128)(2,1)} copy(bf16[32,256,256]{2,1,0:T(8,128)(2,1)} %get-tuple-element.159) | data formatting | bytes 8388608 | tf_op jit(solution)/shard_map
  166.5 5.7 %all-to-all-start = ((f32[8,1,16384]{2,1,0:T(1,128)}), f32[8,1,16384]{2,1,0:T(1,128)S(1)}, u32[]{:S(2)}, u32[]{:S(2)}) async-start(f32[8,1,16384]{2,1,0:T(1,128)} %copy.14), calls=%async_computation | async-start | bytes 1048576 | tf_op jit(solution)/shard_map/all_to_all | solution.py:92
  176.1 6.4 %all-to-all-done = f32[8,1,16384]{2,1,0:T(1,128)S(1)} async-done(((f32[8,1,16384]{2,1,0:T(1,128)}), f32[8,1,16384]{2,1,0:T(1,128)S(1)}, u32[]{:S(2)}, u32[]{:S(2)}) %all-to-all-start) | async-done | bytes 524320 | tf_op jit(solution)/shard_map/all_to_all | solution.py:92
  183.2 31.1 %all-gather = bf16[1024,128]{1,0:T(8,128)(2,1)S(1)} all-gather(bf16[128,128]{1,0:T(8,128)(2,1)S(1)} %fusion.28), channel_id=2, replica_groups=mesh['grp'=4,'dev'=8] {'dev'}, dimensions={0}, use_global_device_ids=true | all-gather | bytes 294912 | tf_op jit(solution)/shard_map/all_gather | solution.py:80
  215.1 97.5 %while.21 = (s32[]{:T(128)}, f32[3,256,256]{2,1,0:T(8,128)S(1)}, bf16[3,256,256]{2,1,0:T(8,128)(2,1)S(1)}, bf16[1,32,256,256]{3,2,1,0:T(8,128)(2,1)}, bf16[32,256,256]{2,1,0:T(8,128)(2,1)}, /*index=5*/s32[]{:T(128)}) while((s32[]{:T(128)}, f32[3,256,256]{2,1,0:T(8,128)S(1)}, bf16[3,256,256]{2,1,0:T(8,128)(2,1)S(1)}, ...), condition=%wide.region_6.7_spmd, body=%wide.region_5.6_spmd.sunk | while | flops 2149580800 | bytes 42336340 | solution.py:82
  215.1 5.5 %fusion.118 = bf16[8192,256]{0,1:T(8,128)(2,1)} fusion(bf16[8192,256]{1,0:T(8,128)(2,1)} %bitcast.222, bf16[3,256,256]{2,1,0:T(8,128)(2,1)S(1)} %get-tuple-element.175, s32[]{:T(128)S(6)} %copy.129), kind=kOutput, calls=%fused_computation.8.clone.1 | convolution fusion | flops 1075838976 | bytes 8519684 | tf_op jit(solution)/shard_map/while/body/eval_jaxpr/dot_general | solution.py:29
  220.6 6.4 %copy.116 = bf16[8192,256]{1,0:T(8,128)(2,1)} copy(bf16[8192,256]{0,1:T(8,128)(2,1)} %fusion.118) | data formatting | bytes 8388608 | tf_op jit(solution)/shard_map/while/body/eval_jaxpr/reshape | solution.py:32
  227.0 7.9 %copy.117 = bf16[32,256,256]{1,0,2:T(8,128)(2,1)} copy(bf16[32,256,256]{2,1,0:T(8,128)(2,1)} %bitcast.225) | data formatting | bytes 8388608 | tf_op jit(solution)/shard_map/while/body/eval_jaxpr/reshape | solution.py:32
  234.9 7.9 %copy.118 = bf16[32,256,256]{1,0,2:T(8,128)(2,1)} copy(bf16[32,256,256]{2,1,0:T(8,128)(2,1)} %get-tuple-element.177) | data formatting | bytes 8388608 | tf_op jit(solution)/shard_map
  247.6 5.5 %fusion.118 = bf16[8192,256]{0,1:T(8,128)(2,1)} fusion(bf16[8192,256]{1,0:T(8,128)(2,1)} %bitcast.222, bf16[3,256,256]{2,1,0:T(8,128)(2,1)S(1)} %get-tuple-element.175, s32[]{:T(128)S(6)} %copy.129), kind=kOutput, calls=%fused_computation.8.clone.1 | convolution fusion | flops 1075838976 | bytes 8519684 | tf_op jit(solution)/shard_map/while/body/eval_jaxpr/dot_general | solution.py:29
  253.1 6.4 %copy.116 = bf16[8192,256]{1,0:T(8,128)(2,1)} copy(bf16[8192,256]{0,1:T(8,128)(2,1)} %fusion.118) | data formatting | bytes 8388608 | tf_op jit(solution)/shard_map/while/body/eval_jaxpr/reshape | solution.py:32
  259.5 7.9 %copy.117 = bf16[32,256,256]{1,0,2:T(8,128)(2,1)} copy(bf16[32,256,256]{2,1,0:T(8,128)(2,1)} %bitcast.225) | data formatting | bytes 8388608 | tf_op jit(solution)/shard_map/while/body/eval_jaxpr/reshape | solution.py:32
  267.4 7.9 %copy.118 = bf16[32,256,256]{1,0,2:T(8,128)(2,1)} copy(bf16[32,256,256]{2,1,0:T(8,128)(2,1)} %get-tuple-element.177) | data formatting | bytes 8388608 | tf_op jit(solution)/shard_map
  280.1 5.5 %fusion.118 = bf16[8192,256]{0,1:T(8,128)(2,1)} fusion(bf16[8192,256]{1,0:T(8,128)(2,1)} %bitcast.222, bf16[3,256,256]{2,1,0:T(8,128)(2,1)S(1)} %get-tuple-element.175, s32[]{:T(128)S(6)} %copy.129), kind=kOutput, calls=%fused_computation.8.clone.1 | convolution fusion | flops 1075838976 | bytes 8519684 | tf_op jit(solution)/shard_map/while/body/eval_jaxpr/dot_general | solution.py:29
  285.6 6.4 %copy.116 = bf16[8192,256]{1,0:T(8,128)(2,1)} copy(bf16[8192,256]{0,1:T(8,128)(2,1)} %fusion.118) | data formatting | bytes 8388608 | tf_op jit(solution)/shard_map/while/body/eval_jaxpr/reshape | solution.py:32
  292.0 7.9 %copy.117 = bf16[32,256,256]{1,0,2:T(8,128)(2,1)} copy(bf16[32,256,256]{2,1,0:T(8,128)(2,1)} %bitcast.225) | data formatting | bytes 8388608 | tf_op jit(solution)/shard_map/while/body/eval_jaxpr/reshape | solution.py:32
  299.9 7.9 %copy.118 = bf16[32,256,256]{1,0,2:T(8,128)(2,1)} copy(bf16[32,256,256]{2,1,0:T(8,128)(2,1)} %get-tuple-element.177) | data formatting | bytes 8388608 | tf_op jit(solution)/shard_map
  322.7 6.4 %all-to-all-done.1 = f32[8,1,16384]{2,1,0:T(1,128)S(1)} async-done(((f32[8,1,16384]{2,1,0:T(1,128)}), f32[8,1,16384]{2,1,0:T(1,128)S(1)}, u32[]{:S(2)}, u32[]{:S(2)}) %all-to-all-start.1) | async-done | bytes 524320 | tf_op jit(solution)/shard_map/all_to_all | solution.py:92
  (48 shorter events, 49.2 us)
Async XLA Ops:
  0.0 182.8 %copy-start = (bf16[1,4,128,128]{3,2,1,0:T(8,128)(2,1)S(1)}, bf16[1,4,128,128]{3,2,1,0:T(8,128)(2,1)}, u32[]{:S(2)}) copy-start(bf16[1,4,128,128]{3,2,1,0:T(8,128)(2,1)} %param.16) | copy-start | bytes 393220
  163.8 11.8 %copy-start.1 = (s32[1,4]{1,0:T(1,128)S(1)}, s32[1,4]{1,0:T(1,128)}, u32[]{:S(2)}) copy-start(s32[1,4]{1,0:T(1,128)} %param.21) | copy-start | bytes 52
  163.8 19.0 %copy-start.2 = (f32[1,128,128]{2,1,0:T(8,128)S(1)}, f32[1,128,128]{2,1,0:T(8,128)}, u32[]{:S(2)}) copy-start(f32[1,128,128]{2,1,0:T(8,128)} %param.17) | copy-start | bytes 196612
  163.9 19.0 %copy-start.3 = (f32[1,128]{1,0:T(1,128)S(1)}, f32[1,128]{1,0:T(1,128)}, u32[]{:S(2)}) copy-start(f32[1,128]{1,0:T(1,128)} %param.18) | copy-start | bytes 1540
  166.5 16.0 %all-to-all-start = ((f32[8,1,16384]{2,1,0:T(1,128)}), f32[8,1,16384]{2,1,0:T(1,128)S(1)}, u32[]{:S(2)}, u32[]{:S(2)}) async-start(f32[8,1,16384]{2,1,0:T(1,128)} %copy.14), calls=%async_computation | async-start | bytes 1048576 | tf_op jit(solution)/shard_map/all_to_all | solution.py:92
  172.2 3.4 %collective-permute-start = (bf16[8,128,128]{2,1,0:T(8,128)(2,1)S(1)}, bf16[8,128,128]{2,1,0:T(8,128)(2,1)S(1)}, u32[]{:S(2)}, u32[]{:S(2)}) collective-permute-start(bf16[8,128,128]{2,1,0:T(8,128)(2,1)S(1)} %all_gather.10), channel_id=1, source_target_pairs={{8,0},{16,8},{24,16},{9,1},{17,9},{25,17},{10,2},{18,10},{26,18},{... | collective-permute-start | bytes 786440 | tf_op jit(solution)/shard_map/ppermute | solution.py:13
  315.3 13.8 %all-to-all-start.1 = ((f32[8,1,16384]{2,1,0:T(1,128)}), f32[8,1,16384]{2,1,0:T(1,128)S(1)}, u32[]{:S(2)}, u32[]{:S(2)}) async-start(f32[8,1,16384]{2,1,0:T(1,128)} %copy.15), calls=%async_computation.1 | async-start | bytes 1048576 | tf_op jit(solution)/shard_map/all_to_all | solution.py:92
  318.8 3.4 %collective-permute-start.1 = (bf16[8,128,128]{2,1,0:T(8,128)(2,1)S(1)}, bf16[8,128,128]{2,1,0:T(8,128)(2,1)S(1)}, u32[]{:S(2)}, u32[]{:S(2)}) collective-permute-start(bf16[8,128,128]{2,1,0:T(8,128)(2,1)S(1)} %bitcast.227), channel_id=1, source_target_pairs={{8,0},{16,8},{24,16},{9,1},{17,9},{25,17},{10,2},{18,10},{26,18},{... | collective-permute-start | bytes 786440 | tf_op jit(solution)/shard_map/ppermute | solution.py:13
where the time goes:
time: 334 us; the launch traced here: 330 us
  local copies, waits for them, and re-layouts  136 us (41%)
  blocking collectives  95.4 us (29%)
  matrix products  67.7 us (20%)
  waiting for transfers between devices  16.4 us (5%)
  starting transfers between devices  11.7 us (4%)
    reshape x12, local copies, waits for them, and re-layouts, sandwich(): squeezed = squeezed.reshape(aux_count, pao_width, pao_width)  85.8 us
    all_gather x2, blocking collectives, on_device(): group_amps = lax.all_gather(current, 'dev', axis=0, tiled=True)  64 us
    another operation x8, local copies, waits for them, and re-layouts  47.8 us
    dot_general x6, matrix products, sandwich(): jnp.dot(flat_factor, expanded, preferred_element_type=jnp.float32)  32.8 us
    all_gather x1, blocking collectives, on_device(): group_base = lax.all_gather(bases, 'dev', axis=0, tiled=True)  31.4 us
    dot_general x6, matrix products, sandwich(): jnp.einsum('kad,kbd->ab', squeezed, factor_block, preferred_element_type=...  28.6 us
    all_to_all x2, waiting for transfers between devices, on_device(): lax.all_to_all(spread_terms(selector, terms), 'dev', split_axis=0, concat...  12.8 us
    all_to_all x2, starting transfers between devices, on_device(): lax.all_to_all(spread_terms(selector, terms), 'dev', split_axis=0, concat...  9.17 us
  transfers between devices with their start and end apart: 4, of which 4 were waited for; matrix products, arithmetic and copies ran while one was open for 0% of the time, Pallas kernels for 0%

commit v1 on v0

v1 whole, which is shorter than its diff:
```python
import functools

import jax
import jax.numpy as jnp
from jax import lax
from jax.experimental import pallas as pl
from jax.experimental.pallas import tpu as pltpu
from jax.sharding import PartitionSpec as P

CAP = 3
ITERS = 2
F32 = jnp.float32
BF16 = jnp.bfloat16


def vmem_spec():
    return pl.BlockSpec(memory_space=pltpu.VMEM)


def smem_spec():
    return pl.BlockSpec(memory_space=pltpu.SMEM)


def params(mib):
    return pltpu.CompilerParams(vmem_limit_bytes=mib * 2**20)


def gather_xor(value, axis):
    count = lax.axis_size(axis)
    bit = 1
    blocks = value
    while bit < count:
        other = lax.ppermute(blocks, axis, [(d, d ^ bit) for d in range(count)])
        blocks = jnp.concatenate([blocks, other], axis=0)
        bit *= 2
    return blocks


def from_next(value, axis):
    count = lax.axis_size(axis)
    return lax.ppermute(value, axis, [(d, d - 1) for d in range(1, count)])


def project_kernel(slots, bases_ref, factors_ref, out_ref, wide, narrow, half):
    aux, width, npno = factors_ref.shape[0], bases_ref.shape[1], bases_ref.shape[2]

    @pl.when(pl.program_id(0) == 0)
    def _():
        for s in range(CAP):
            base = bases_ref[slots[s]]
            narrow[s] = base
            wide[pl.ds(s * npno, npno), :] = base.astype(F32).T.astype(BF16)

    for k in range(aux):
        left = jnp.dot(wide[...], factors_ref[k], preferred_element_type=F32).astype(BF16)
        for s in range(CAP):
            half[s, pl.ds(k * npno, npno), :] = left[s * npno : (s + 1) * npno]
    for s in range(CAP):
        both = jnp.dot(half[s], narrow[s], preferred_element_type=F32).astype(BF16)
        for k in range(aux):
            out_ref[s, k // 2, :, pl.ds((k % 2) * npno, npno)] = both[k * npno : (k + 1) * npno]


def project(slots, group_bases, factor_block, step=8):
    aux, width, _ = factor_block.shape
    count, _, npno = group_bases.shape
    step = min(step, aux)
    return pl.pallas_call(
        project_kernel,
        grid=(aux // step,),
        in_specs=[
            smem_spec(),
            pl.BlockSpec((count, width, npno), lambda i: (0, 0, 0)),
            pl.BlockSpec((step, width, width), lambda i: (i, 0, 0)),
        ],
        out_specs=pl.BlockSpec((CAP, step // 2, npno, 2 * npno), lambda i: (0, i, 0, 0)),
        out_shape=jax.ShapeDtypeStruct((CAP, aux // 2, npno, 2 * npno), BF16),
        scratch_shapes=[
            pltpu.VMEM((CAP * npno, width), BF16),
            pltpu.VMEM((CAP, width, npno), BF16),
            pltpu.VMEM((CAP, step * npno, width), BF16),
        ],
        compiler_params=params(48),
        name="project",
    )(slots, group_bases, factor_block)


def ladder_kernel(slots, pairs, amps_ref, proj_ref, out_ref, twice, mixed):
    half, npno = proj_ref.shape[1], proj_ref.shape[2]
    out_ref[...] = jnp.zeros_like(out_ref)
    twice[...] = jnp.zeros_like(twice)
    for s in range(CAP):
        amp = amps_ref[slots[s]]
        twice[pl.ds(0, npno), pl.ds(0, npno)] = amp
        twice[pl.ds(npno, npno), pl.ds(npno, npno)] = amp
        flat = proj_ref[s].reshape(half * npno, 2 * npno)
        mixed[...] = jnp.dot(flat, twice[...], preferred_element_type=F32).astype(BF16)
        total = jnp.zeros((npno, npno), F32)
        for m in range(half):
            total = total + lax.dot_general(
                mixed[pl.ds(m * npno, npno), :],
                proj_ref[s, m],
                (((1,), (1,)), ((), ())),
                preferred_element_type=F32,
            )

        @pl.when(pairs[s] >= 0)
        def _():
            out_ref[jnp.maximum(pairs[s], 0)] = total.astype(BF16)


def ladder(slots, pairs, group_amps, projected):
    count, npno, _ = group_amps.shape
    half = projected.shape[1]
    return pl.pallas_call(
        ladder_kernel,
        in_specs=[smem_spec(), smem_spec(), vmem_spec(), vmem_spec()],
        out_specs=vmem_spec(),
        out_shape=jax.ShapeDtypeStruct((count, npno, npno), BF16),
        scratch_shapes=[
            pltpu.VMEM((2 * npno, 2 * npno), BF16),
            pltpu.VMEM((half * npno, 2 * npno), BF16),
        ],
        compiler_params=params(32),
        name="ladder",
    )(slots, pairs, group_amps, projected)


def coupling_kernel(near, own_ref, next_ref, inter_ref, ints_ref, out_ref):
    count = own_ref.shape[0]
    total = ints_ref[...]
    for n in range(inter_ref.shape[0]):
        at = near[n]
        own = own_ref[jnp.minimum(at, count - 1)]
        far = next_ref[jnp.maximum(at - count, 0)]
        amp = jnp.where(at < count, own, far)
        inter = inter_ref[n]
        mixed = jnp.dot(inter, amp, preferred_element_type=F32).astype(BF16)
        total = total + lax.dot_general(
            mixed, inter, (((1,), (1,)), ((), ())), preferred_element_type=F32
        )
    out_ref[...] = total


def coupling(near, own, following, inter, ints):
    return pl.pallas_call(
        coupling_kernel,
        in_specs=[smem_spec()] + [vmem_spec()] * 4,
        out_specs=vmem_spec(),
        out_shape=jax.ShapeDtypeStruct(ints.shape, F32),
        compiler_params=params(32),
        name="coupling",
    )(near, own, following, inter, ints)


def update_kernel(atoms, rest_ref, terms_ref, across_ref, down_ref, shift, out_ref):
    total = rest_ref[...]
    for j in range(atoms.shape[0]):
        total = total + terms_ref[atoms[j]].astype(F32)
    denominator = down_ref[...] + across_ref[...] + shift[0]
    out_ref[...] = (-total / denominator).astype(out_ref.dtype)


def update_pair(atoms, rest, terms, across, down, shift, dtype):
    return pl.pallas_call(
        update_kernel,
        in_specs=[smem_spec()] + [vmem_spec()] * 4 + [smem_spec()],
        out_specs=vmem_spec(),
        out_shape=jax.ShapeDtypeStruct(rest.shape, dtype),
        compiler_params=params(32),
        name="update",
    )(atoms, rest, terms, across, down, shift)


def on_device(
    amplitudes,
    bases,
    factors,
    intersections,
    pair_integrals,
    pno_energies,
    pair_shift,
    pair_atoms,
    pair_next,
):
    me = lax.axis_index("dev")
    count = lax.axis_size("dev")
    listed = jnp.any(pair_atoms == me, axis=1)
    order = jnp.sort(jnp.where(listed, jnp.arange(count), count))[:CAP].astype(jnp.int32)
    pairs = jnp.where(order < count, order, -1)
    slots = jnp.where(order < count, order ^ me, 0)
    near = pair_next[0]
    near = jnp.where(near < count, near ^ me, ((near - count) ^ me) + count)
    atoms = pair_atoms[me]
    across = pno_energies
    down = pno_energies.reshape(-1, 1)
    inter = intersections[0]
    ints = pair_integrals[0]

    group_bases = gather_xor(bases, "dev")
    group_amps = gather_xor(amplitudes, "dev")
    projected = project(slots, group_bases, factors[0])
    for iteration in range(ITERS):
        terms = ladder(slots, pairs, group_amps, projected)
        arrived = lax.all_to_all(terms, "dev", split_axis=0, concat_axis=0, tiled=True)
        next_amps = from_next(group_amps, "grp")
        rest = coupling(near, group_amps, next_amps, inter, ints)
        last = iteration + 1 == ITERS
        update = update_pair(
            atoms, rest, arrived, across, down, pair_shift, F32 if last else BF16
        )
        if not last:
            group_amps = gather_xor(update[None], "dev")
    return update[None]


def solution(mesh):
    return jax.shard_map(
        on_device,
        mesh=mesh,
        in_specs=(
            P(("grp", "dev"), None, None),
            P(("grp", "dev"), None, None),
            P(("grp", "dev"), None, None, None),
            P(("grp", "dev"), None, None, None),
            P(("grp", "dev"), None, None),
            P(("grp", "dev"), None),
            P(("grp", "dev")),
            P("grp", None),
            P(("grp", "dev"), None),
        ),
        out_specs=P(("grp", "dev"), None, None),
        check_vma=False,
    )
```

time: 334 us -> 95.2 us (0.29)
  the two profiles are of different devices: /device:TPU:0 before, /device:TPU:1 now
where the time goes in v1:
time: 95.2 us; the launch traced here: 94.2 us
  waiting for transfers between devices  35 us (37%)
  starting transfers between devices  29.6 us (31%)
  Pallas kernels  16.9 us (18%)
  local copies, waits for them, and re-layouts  6.01 us (6%)
  other arithmetic  5.88 us (6%)
    ppermute x9, waiting for transfers between devices, gather_xor(): other = lax.ppermute(blocks, axis, [(d, d ^ bit) for d in range(count)])  25 us
    ppermute x9, starting transfers between devices, gather_xor(): other = lax.ppermute(blocks, axis, [(d, d ^ bit) for d in range(count)])  14.3 us
    ppermute x2, waiting for transfers between devices, from_next(): return lax.ppermute(value, axis, [(d, d - 1) for d in range(1, count)])  9.93 us
    all_to_all x2, starting transfers between devices, on_device(): lax.all_to_all(terms, 'dev', split_axis=0, concat_axis=0, tiled=True)  8.9 us
    ppermute x2, starting transfers between devices, from_next(): return lax.ppermute(value, axis, [(d, d - 1) for d in range(1, count)])  6.42 us
    pallas_call x2, Pallas kernels, ladder(): pl.pallas_call(ladder_kernel, in_specs=[smem_spec(), smem_spec(), vmem_sp...  6.31 us
    pallas_call x1, Pallas kernels, project(): pl.pallas_call(project_kernel, grid=(aux // step,), in_specs=[smem_spec()...  5.8 us
    unnamed x25, local copies, waits for them, and re-layouts  5.69 us
  transfers between devices with their start and end apart: 13, of which 8 were waited for; matrix products, arithmetic and copies ran while one was open for 6% of the time, Pallas kernels for 3%

profile of v1, /device:TPU:1, one launch (start us, length us, event | category | flops | bytes accessed | tf_op | source)
XLA Modules:
  0.0 94.2 jit_solution(12209783943351759556)
XLA Ops:
  0.0 2.1 %collective-permute-start.4 = (bf16[1,256,128]{2,1,0:T(8,128)(2,1)}, bf16[1,256,128]{2,1,0:T(8,128)(2,1)S(1)}, u32[]{:S(2)}, u32[]{:S(2)}) collective-permute-start(bf16[1,256,128]{2,1,0:T(8,128)(2,1)} %param.10), channel_id=1, source_target_pairs={{0,1},{1,0},{2,3},{3,2},{4,5},{5,4},{6,7},{7,6},{8,9},{9,8},{10,11... | collective-permute-start | bytes 196616 | tf_op jit(solution)/shard_map/ppermute | solution.py:33
  2.8 1.0 %sort.15 = (s32[8]{0:T(128)S(1)}, s32[8]{0:T(128)}) sort(s32[8]{0:T(128)S(1)} %iota_select_fusion, s32[8]{0:T(128)S(1)} %iota.7), dimensions={0}, to_apply=%region_1.2 | sort | flops 24 | bytes 128 | tf_op jit(solution)/shard_map/jit(sort)/sort | solution.py:189
  3.8 1.4 %collective-permute-done = bf16[1,128,128]{2,1,0:T(8,128)(2,1)S(1)} collective-permute-done((bf16[1,128,128]{2,1,0:T(8,128)(2,1)}, bf16[1,128,128]{2,1,0:T(8,128)(2,1)S(1)}, u32[]{:S(2)}, u32[]{:S(2)}) %collective-permute-start) | collective-permute-done | bytes 32800 | tf_op jit(solution)/shard_map/ppermute | solution.py:33
  6.0 1.8 %collective-permute-start.1 = (bf16[2,128,128]{2,1,0:T(8,128)(2,1)S(1)}, bf16[2,128,128]{2,1,0:T(8,128)(2,1)S(1)}, u32[]{:S(2)}, u32[]{:S(2)}) collective-permute-start(bf16[2,128,128]{2,1,0:T(8,128)(2,1)S(1)} %pad_maximum_fusion.6), channel_id=1, source_target_pairs={{0,2},{1,3},{2,0},{3,1},{4,6},{5,7},{6,4},{7,5},{8,10},{9,11},{10,... | collective-permute-start | bytes 196616 | tf_op jit(solution)/shard_map/ppermute | solution.py:33
  7.8 0.9 pad_maximum_fusion.4
  10.2 2.5 %collective-permute-start.2 = (bf16[4,128,128]{2,1,0:T(8,128)(2,1)S(1)}, bf16[4,128,128]{2,1,0:T(8,128)(2,1)S(1)}, u32[]{:S(2)}, u32[]{:S(2)}) collective-permute-start(bf16[4,128,128]{2,1,0:T(8,128)(2,1)S(1)} %pad_maximum_fusion.3), channel_id=1, source_target_pairs={{0,4},{1,5},{2,6},{3,7},{4,0},{5,1},{6,2},{7,3},{8,12},{9,13},{10,... | collective-permute-start | bytes 393224 | tf_op jit(solution)/shard_map/ppermute | solution.py:33
  12.9 0.9 pad_maximum_fusion.1
  13.8 2.4 %collective-permute-start.6 = (bf16[4,256,128]{2,1,0:T(8,128)(2,1)S(1)}, bf16[4,256,128]{2,1,0:T(8,128)(2,1)S(1)}, u32[]{:S(2)}, u32[]{:S(2)}) collective-permute-start(bf16[4,256,128]{2,1,0:T(8,128)(2,1)S(1)} %pad_maximum_fusion.1), channel_id=1, source_target_pairs={{0,4},{1,5},{2,6},{3,7},{4,0},{5,1},{6,2},{7,3},{8,12},{9,13},{10,... | collective-permute-start | bytes 786440 | tf_op jit(solution)/shard_map/ppermute | solution.py:33
  16.2 13.9 %collective-permute-done.6 = bf16[4,256,128]{2,1,0:T(8,128)(2,1)S(1)} collective-permute-done((bf16[4,256,128]{2,1,0:T(8,128)(2,1)S(1)}, bf16[4,256,128]{2,1,0:T(8,128)(2,1)S(1)}, u32[]{:S(2)}, u32[]{:S(2)}) %collective-permute-start.6) | collective-permute-done | bytes 262176 | tf_op jit(solution)/shard_map/ppermute | solution.py:33
  30.1 0.9 pad_maximum_fusion.bases_ref
  31.1 5.8 %project.1.proj_ref = bf16[3,16,128,256]{3,2,1,0:T(8,128)(2,1)S(1)} custom-call(s32[3]{0:T(128)S(1)} %get-tuple-element.9.slots, bf16[8,256,128]{2,1,0:T(8,128)(2,1)S(1)} %pad_maximum_fusion.bases_ref, bf16[32,256,256]{2,1,0:T(8,128)(2,1)} %bitcast.17), custom_call_target="tpu_custom_call" | custom-call | tf_op jit(solution)/shard_map/project/pallas_call | solution.py:68
  36.9 3.2 %ladder.2 = bf16[8,128,128]{2,1,0:T(8,128)(2,1)S(1)} custom-call(s32[3]{0:T(128)S(1)} %get-tuple-element.9.slots, s32[3]{0:T(128)S(1)} %get-tuple-element.8.pairs, bf16[8,128,128]{2,1,0:T(8,128)(2,1)S(1)} %constant_dynamic-update-slice_fusion.own_ref.amps_ref, bf16[3,16,128,256]{3,2,1,0:T(8,128)(2,1)S(1)} %project.1.proj_ref), custom_call_target="tpu_custom_call" | custom-call | tf_op jit(solution)/shard_map/ladder/pallas_call | solution.py:115
  40.7 4.0 %all-to-all-start = ((bf16[8,128,128]{2,1,0:T(8,128)(2,1)}), bf16[8,128,128]{2,1,0:T(8,128)(2,1)}, u32[]{:S(2)}, u32[]{:S(2)}) async-start(bf16[8,128,128]{2,1,0:T(8,128)(2,1)} %copy-done), calls=%async_computation | async-start | bytes 524288 | tf_op jit(solution)/shard_map/all_to_all | solution.py:205
  44.8 3.8 %collective-permute-start.3 = (bf16[8,128,128]{2,1,0:T(8,128)(2,1)S(1)}, bf16[8,128,128]{2,1,0:T(8,128)(2,1)}, u32[]{:S(2)}, u32[]{:S(2)}) collective-permute-start(bf16[8,128,128]{2,1,0:T(8,128)(2,1)S(1)} %constant_dynamic-update-slice_fusion.own_ref.amps_ref), channel_id=1, source_target_pairs={{8,0},{16,8},{24,16},{9,1},{17,9},{25,17},{10,2},{18,10},{26,18},{... | collective-permute-start | bytes 786440 | tf_op jit(solution)/shard_map/ppermute | solution.py:41
  49.6 4.5 %collective-permute-done.3.next_ref = bf16[8,128,128]{2,1,0:T(8,128)(2,1)} collective-permute-done((bf16[8,128,128]{2,1,0:T(8,128)(2,1)S(1)}, bf16[8,128,128]{2,1,0:T(8,128)(2,1)}, u32[]{:S(2)}, u32[]{:S(2)}) %collective-permute-start.3) | collective-permute-done | bytes 262176 | tf_op jit(solution)/shard_map/ppermute | solution.py:41
  54.2 0.9 copy-done.2
  55.1 0.8 copy-done.4
  55.9 1.4 %coupling.2.rest_ref = f32[128,128]{1,0:T(8,128)S(1)} custom-call(s32[4]{0:T(128)S(1)} %fusion.near, bf16[8,128,128]{2,1,0:T(8,128)(2,1)S(1)} %constant_dynamic-update-slice_fusion.own_ref.amps_ref, bf16[8,128,128]{2,1,0:T(8,128)(2,1)} %collective-permute-done.3.next_ref, bf16[4,128,128]{2,1,0:T(8,128)(2,1)S(1)} %bitcast.8, f32[128,128]{1,0:T(8,128)S(1)} %bitcast.14), custom_call_target="tpu_custom_call" | custom-call | tf_op jit(solution)/shard_map/coupling/pallas_call | solution.py:146
  57.4 1.1 %update.2 = bf16[128,128]{1,0:T(8,128)(2,1)S(1)} custom-call(s32[2]{0:T(128)S(1)} %dynamic-slice_reduce_fusion.atoms, f32[128,128]{1,0:T(8,128)S(1)} %coupling.2.rest_ref, bf16[8,128,128]{2,1,0:T(8,128)(2,1)} %all-to-all-done.terms_ref, f32[1,128]{1,0:T(1,128)S(1)} %copy-done.6, f32[128,1]{1,0:T(8,128)S(1)} %copy.10.down_ref, f32[1]{0:T(128)S(6)} %copy.15.shift), custom_call_target="tpu_custom_call" | custom-call | tf_op jit(solution)/shard_map/update/pallas_call | solution.py:165
  58.4 1.5 %collective-permute-start.7 = (bf16[1,128,128]{2,1,0:T(8,128)(2,1)S(1)}, bf16[1,128,128]{2,1,0:T(8,128)(2,1)S(1)}, u32[]{:S(2)}, u32[]{:S(2)}) collective-permute-start(bf16[1,128,128]{2,1,0:T(8,128)(2,1)S(1)} %bitcast.10), channel_id=1, source_target_pairs={{0,1},{1,0},{2,3},{3,2},{4,5},{5,4},{6,7},{7,6},{8,9},{9,8},{10,11... | collective-permute-start | bytes 98312 | tf_op jit(solution)/shard_map/ppermute | solution.py:33
  60.0 1.3 %collective-permute-done.7 = bf16[1,128,128]{2,1,0:T(8,128)(2,1)S(1)} collective-permute-done((bf16[1,128,128]{2,1,0:T(8,128)(2,1)S(1)}, bf16[1,128,128]{2,1,0:T(8,128)(2,1)S(1)}, u32[]{:S(2)}, u32[]{:S(2)}) %collective-permute-start.7) | collective-permute-done | bytes 32800 | tf_op jit(solution)/shard_map/ppermute | solution.py:33
  61.3 1.5 %collective-permute-start.8 = (bf16[2,128,128]{2,1,0:T(8,128)(2,1)S(1)}, bf16[2,128,128]{2,1,0:T(8,128)(2,1)S(1)}, u32[]{:S(2)}, u32[]{:S(2)}) collective-permute-start(bf16[2,128,128]{2,1,0:T(8,128)(2,1)S(1)} %pad_maximum_fusion.7), channel_id=1, source_target_pairs={{0,2},{1,3},{2,0},{3,1},{4,6},{5,7},{6,4},{7,5},{8,10},{9,11},{10,... | collective-permute-start | bytes 196616 | tf_op jit(solution)/shard_map/ppermute | solution.py:33
  62.8 1.7 %collective-permute-done.8 = bf16[2,128,128]{2,1,0:T(8,128)(2,1)S(1)} collective-permute-done((bf16[2,128,128]{2,1,0:T(8,128)(2,1)S(1)}, bf16[2,128,128]{2,1,0:T(8,128)(2,1)S(1)}, u32[]{:S(2)}, u32[]{:S(2)}) %collective-permute-start.8) | collective-permute-done | bytes 65568 | tf_op jit(solution)/shard_map/ppermute | solution.py:33
  64.5 2.4 %collective-permute-start.9 = (bf16[4,128,128]{2,1,0:T(8,128)(2,1)S(1)}, bf16[4,128,128]{2,1,0:T(8,128)(2,1)S(1)}, u32[]{:S(2)}, u32[]{:S(2)}) collective-permute-start(bf16[4,128,128]{2,1,0:T(8,128)(2,1)S(1)} %pad_maximum_fusion.5), channel_id=1, source_target_pairs={{0,4},{1,5},{2,6},{3,7},{4,0},{5,1},{6,2},{7,3},{8,12},{9,13},{10,... | collective-permute-start | bytes 393224 | tf_op jit(solution)/shard_map/ppermute | solution.py:33
  66.9 6.5 %collective-permute-done.9 = bf16[4,128,128]{2,1,0:T(8,128)(2,1)S(1)} collective-permute-done((bf16[4,128,128]{2,1,0:T(8,128)(2,1)S(1)}, bf16[4,128,128]{2,1,0:T(8,128)(2,1)S(1)}, u32[]{:S(2)}, u32[]{:S(2)}) %collective-permute-start.9) | collective-permute-done | bytes 131104 | tf_op jit(solution)/shard_map/ppermute | solution.py:33
  73.5 3.2 %ladder.3 = bf16[8,128,128]{2,1,0:T(8,128)(2,1)S(1)} custom-call(s32[3]{0:T(128)S(1)} %get-tuple-element.9.slots, s32[3]{0:T(128)S(1)} %get-tuple-element.8.pairs, bf16[8,128,128]{2,1,0:T(8,128)(2,1)S(1)} %pad_maximum_fusion.2.own_ref.amps_ref, bf16[3,16,128,256]{3,2,1,0:T(8,128)(2,1)S(1)} %project.1.proj_ref), custom_call_target="tpu_custom_call" | custom-call | tf_op jit(solution)/shard_map/ladder/pallas_call | solution.py:115
  77.3 4.9 %all-to-all-start.1 = ((bf16[8,128,128]{2,1,0:T(8,128)(2,1)}), bf16[8,128,128]{2,1,0:T(8,128)(2,1)S(1)}, u32[]{:S(2)}, u32[]{:S(2)}) async-start(bf16[8,128,128]{2,1,0:T(8,128)(2,1)} %copy-done.1), calls=%async_computation.1 | async-start | bytes 524288 | tf_op jit(solution)/shard_map/all_to_all | solution.py:205
  82.2 2.6 %collective-permute-start.10 = (bf16[8,128,128]{2,1,0:T(8,128)(2,1)S(1)}, bf16[8,128,128]{2,1,0:T(8,128)(2,1)S(1)}, u32[]{:S(2)}, u32[]{:S(2)}) collective-permute-start(bf16[8,128,128]{2,1,0:T(8,128)(2,1)S(1)} %pad_maximum_fusion.2.own_ref.amps_ref), channel_id=1, source_target_pairs={{8,0},{16,8},{24,16},{9,1},{17,9},{25,17},{10,2},{18,10},{26,18},{... | collective-permute-start | bytes 786440 | tf_op jit(solution)/shard_map/ppermute | solution.py:41
  84.8 5.4 %collective-permute-done.10.next_ref = bf16[8,128,128]{2,1,0:T(8,128)(2,1)S(1)} collective-permute-done((bf16[8,128,128]{2,1,0:T(8,128)(2,1)S(1)}, bf16[8,128,128]{2,1,0:T(8,128)(2,1)S(1)}, u32[]{:S(2)}, u32[]{:S(2)}) %collective-permute-start.10) | collective-permute-done | bytes 262176 | tf_op jit(solution)/shard_map/ppermute | solution.py:41
  90.2 0.9 copy-done.3
  91.9 1.0 %coupling.3.rest_ref = f32[128,128]{1,0:T(8,128)S(1)} custom-call(s32[4]{0:T(128)S(1)} %copy-done.8, bf16[8,128,128]{2,1,0:T(8,128)(2,1)S(1)} %pad_maximum_fusion.2.own_ref.amps_ref, bf16[8,128,128]{2,1,0:T(8,128)(2,1)S(1)} %collective-permute-done.10.next_ref, bf16[4,128,128]{2,1,0:T(8,128)(2,1)S(1)} %bitcast.9, f32[128,128]{1,0:T(8,128)S(1)} %bitcast.15), custom_call_target="tpu_custom_call" | custom-call | tf_op jit(solution)/shard_map/coupling/pallas_call | solution.py:146
  92.9 1.3 %update.3 = f32[128,128]{1,0:T(8,128)} custom-call(s32[2]{0:T(128)S(1)} %dynamic-slice_reduce_fusion.atoms, f32[128,128]{1,0:T(8,128)S(1)} %coupling.3.rest_ref, bf16[8,128,128]{2,1,0:T(8,128)(2,1)S(1)} %all-to-all-done.1.terms_ref, f32[1,128]{1,0:T(1,128)S(1)} %copy-done.6, f32[128,1]{1,0:T(8,128)S(1)} %copy.10.down_ref, f32[1]{0:T(128)S(6)} %copy.15.shift), custom_call_target="tpu_custom_call" | custom-call | tf_op jit(solution)/shard_map/update/pallas_call | solution.py:165
  (43 shorter events, 5.9 us)
Async XLA Ops:
  0.0 7.8 %collective-permute-start.4 = (bf16[1,256,128]{2,1,0:T(8,128)(2,1)}, bf16[1,256,128]{2,1,0:T(8,128)(2,1)S(1)}, u32[]{:S(2)}, u32[]{:S(2)}) collective-permute-start(bf16[1,256,128]{2,1,0:T(8,128)(2,1)} %param.10), channel_id=1, source_target_pairs={{0,1},{1,0},{2,3},{3,2},{4,5},{5,4},{6,7},{7,6},{8,9},{9,8},{10,11... | collective-permute-start | bytes 196616 | tf_op jit(solution)/shard_map/ppermute | solution.py:33
  2.1 3.2 %collective-permute-start = (bf16[1,128,128]{2,1,0:T(8,128)(2,1)}, bf16[1,128,128]{2,1,0:T(8,128)(2,1)S(1)}, u32[]{:S(2)}, u32[]{:S(2)}) collective-permute-start(bf16[1,128,128]{2,1,0:T(8,128)(2,1)} %param.9), channel_id=1, source_target_pairs={{0,1},{1,0},{2,3},{3,2},{4,5},{5,4},{6,7},{7,6},{8,9},{9,8},{10,11... | collective-permute-start | bytes 98312 | tf_op jit(solution)/shard_map/ppermute | solution.py:33
  6.0 3.5 %collective-permute-start.1 = (bf16[2,128,128]{2,1,0:T(8,128)(2,1)S(1)}, bf16[2,128,128]{2,1,0:T(8,128)(2,1)S(1)}, u32[]{:S(2)}, u32[]{:S(2)}) collective-permute-start(bf16[2,128,128]{2,1,0:T(8,128)(2,1)S(1)} %pad_maximum_fusion.6), channel_id=1, source_target_pairs={{0,2},{1,3},{2,0},{3,1},{4,6},{5,7},{6,4},{7,5},{8,10},{9,11},{10,... | collective-permute-start | bytes 196616 | tf_op jit(solution)/shard_map/ppermute | solution.py:33
  8.6 4.3 %collective-permute-start.5 = (bf16[2,256,128]{2,1,0:T(8,128)(2,1)S(1)}, bf16[2,256,128]{2,1,0:T(8,128)(2,1)S(1)}, u32[]{:S(2)}, u32[]{:S(2)}) collective-permute-start(bf16[2,256,128]{2,1,0:T(8,128)(2,1)S(1)} %pad_maximum_fusion.4), channel_id=1, source_target_pairs={{0,2},{1,3},{2,0},{3,1},{4,6},{5,7},{6,4},{7,5},{8,10},{9,11},{10,... | collective-permute-start | bytes 393224 | tf_op jit(solution)/shard_map/ppermute | solution.py:33
  10.2 5.9 %collective-permute-start.2 = (bf16[4,128,128]{2,1,0:T(8,128)(2,1)S(1)}, bf16[4,128,128]{2,1,0:T(8,128)(2,1)S(1)}, u32[]{:S(2)}, u32[]{:S(2)}) collective-permute-start(bf16[4,128,128]{2,1,0:T(8,128)(2,1)S(1)} %pad_maximum_fusion.3), channel_id=1, source_target_pairs={{0,4},{1,5},{2,6},{3,7},{4,0},{5,1},{6,2},{7,3},{8,12},{9,13},{10,... | collective-permute-start | bytes 393224 | tf_op jit(solution)/shard_map/ppermute | solution.py:33
  13.8 16.4 %collective-permute-start.6 = (bf16[4,256,128]{2,1,0:T(8,128)(2,1)S(1)}, bf16[4,256,128]{2,1,0:T(8,128)(2,1)S(1)}, u32[]{:S(2)}, u32[]{:S(2)}) collective-permute-start(bf16[4,256,128]{2,1,0:T(8,128)(2,1)S(1)} %pad_maximum_fusion.1), channel_id=1, source_target_pairs={{0,4},{1,5},{2,6},{3,7},{4,0},{5,1},{6,2},{7,3},{8,12},{9,13},{10,... | collective-permute-start | bytes 786440 | tf_op jit(solution)/shard_map/ppermute | solution.py:33
  31.0 17.6 %copy-start.9 = (s32[8,2]{0,1:T(2,128)S(1)}, s32[8,2]{0,1:T(2,128)}, u32[]{:S(2)}) copy-start(s32[8,2]{0,1:T(2,128)} %param.16) | copy-start | bytes 196
  31.0 17.8 %copy-start.6 = (f32[1,128]{1,0:T(1,128)S(1)}, f32[1,128]{1,0:T(1,128)}, u32[]{:S(2)}) copy-start(f32[1,128]{1,0:T(1,128)} %across_ref.3) | copy-start | bytes 1540
  31.0 18.6 %copy-start.10 = (s32[1,4]{1,0:T(1,128)S(1)}, s32[1,4]{1,0:T(1,128)}, u32[]{:S(2)}) copy-start(s32[1,4]{1,0:T(1,128)} %param.17) | copy-start | bytes 52
  40.0 0.7 copy-start
  40.7 16.6 %all-to-all-start = ((bf16[8,128,128]{2,1,0:T(8,128)(2,1)}), bf16[8,128,128]{2,1,0:T(8,128)(2,1)}, u32[]{:S(2)}, u32[]{:S(2)}) async-start(bf16[8,128,128]{2,1,0:T(8,128)(2,1)} %copy-done), calls=%async_computation | async-start | bytes 524288 | tf_op jit(solution)/shard_map/all_to_all | solution.py:205
  44.8 9.4 %collective-permute-start.3 = (bf16[8,128,128]{2,1,0:T(8,128)(2,1)S(1)}, bf16[8,128,128]{2,1,0:T(8,128)(2,1)}, u32[]{:S(2)}, u32[]{:S(2)}) collective-permute-start(bf16[8,128,128]{2,1,0:T(8,128)(2,1)S(1)} %constant_dynamic-update-slice_fusion.own_ref.amps_ref), channel_id=1, source_target_pairs={{8,0},{16,8},{24,16},{9,1},{17,9},{25,17},{10,2},{18,10},{26,18},{... | collective-permute-start | bytes 786440 | tf_op jit(solution)/shard_map/ppermute | solution.py:41
  49.6 4.5 %copy-start.7 = (s32[4]{0:T(128)}, s32[4]{0:T(128)S(1)}, u32[]{:S(2)}) copy-start(s32[4]{0:T(128)S(1)} %fusion.near) | copy-start | bytes 52
  54.2 0.9 copy-start.2
  55.1 0.8 copy-start.4
  58.4 31.7 %copy-start.8 = (s32[4]{0:T(128)S(1)}, s32[4]{0:T(128)}, u32[]{:S(2)}) copy-start(s32[4]{0:T(128)} %copy-done.7) | copy-start | bytes 52
  58.4 2.8 %collective-permute-start.7 = (bf16[1,128,128]{2,1,0:T(8,128)(2,1)S(1)}, bf16[1,128,128]{2,1,0:T(8,128)(2,1)S(1)}, u32[]{:S(2)}, u32[]{:S(2)}) collective-permute-start(bf16[1,128,128]{2,1,0:T(8,128)(2,1)S(1)} %bitcast.10), channel_id=1, source_target_pairs={{0,1},{1,0},{2,3},{3,2},{4,5},{5,4},{6,7},{7,6},{8,9},{9,8},{10,11... | collective-permute-start | bytes 98312 | tf_op jit(solution)/shard_map/ppermute | solution.py:33
  61.3 3.2 %collective-permute-start.8 = (bf16[2,128,128]{2,1,0:T(8,128)(2,1)S(1)}, bf16[2,128,128]{2,1,0:T(8,128)(2,1)S(1)}, u32[]{:S(2)}, u32[]{:S(2)}) collective-permute-start(bf16[2,128,128]{2,1,0:T(8,128)(2,1)S(1)} %pad_maximum_fusion.7), channel_id=1, source_target_pairs={{0,2},{1,3},{2,0},{3,1},{4,6},{5,7},{6,4},{7,5},{8,10},{9,11},{10,... | collective-permute-start | bytes 196616 | tf_op jit(solution)/shard_map/ppermute | solution.py:33
  64.5 8.9 %collective-permute-start.9 = (bf16[4,128,128]{2,1,0:T(8,128)(2,1)S(1)}, bf16[4,128,128]{2,1,0:T(8,128)(2,1)S(1)}, u32[]{:S(2)}, u32[]{:S(2)}) collective-permute-start(bf16[4,128,128]{2,1,0:T(8,128)(2,1)S(1)} %pad_maximum_fusion.5), channel_id=1, source_target_pairs={{0,4},{1,5},{2,6},{3,7},{4,0},{5,1},{6,2},{7,3},{8,12},{9,13},{10,... | collective-permute-start | bytes 393224 | tf_op jit(solution)/shard_map/ppermute | solution.py:33
  76.6 0.7 copy-start.1
  77.3 15.6 %all-to-all-start.1 = ((bf16[8,128,128]{2,1,0:T(8,128)(2,1)}), bf16[8,128,128]{2,1,0:T(8,128)(2,1)S(1)}, u32[]{:S(2)}, u32[]{:S(2)}) async-start(bf16[8,128,128]{2,1,0:T(8,128)(2,1)} %copy-done.1), calls=%async_computation.1 | async-start | bytes 524288 | tf_op jit(solution)/shard_map/all_to_all | solution.py:205
  82.2 8.0 %collective-permute-start.10 = (bf16[8,128,128]{2,1,0:T(8,128)(2,1)S(1)}, bf16[8,128,128]{2,1,0:T(8,128)(2,1)S(1)}, u32[]{:S(2)}, u32[]{:S(2)}) collective-permute-start(bf16[8,128,128]{2,1,0:T(8,128)(2,1)S(1)} %pad_maximum_fusion.2.own_ref.amps_ref), channel_id=1, source_target_pairs={{8,0},{16,8},{24,16},{9,1},{17,9},{25,17},{10,2},{18,10},{26,18},{... | collective-permute-start | bytes 786440 | tf_op jit(solution)/shard_map/ppermute | solution.py:41
  90.2 0.9 copy-start.3
  91.1 0.8 copy-start.5
